TPU v7x, 512 devices: a whole 4x4x16 slice. The times are simulated.
512 devices in a mesh: section: 16 (over z), tp: 8 (over x, core), rep: 4 (over y).
Axes of the slice: x: 4, y: 4, z: 16, core: 2. Of those that a mesh axis runs over, the one named last changes fastest.
Arguments:
- pool: bfloat16 [512, 128, 2, 2048], P(('rep', 'section', 'tp')), parts along dimension 0, may hold values from -6 to 6
- queries: bfloat16 [16, 32, 16384], P('section', 'rep', 'tp'), parts along dimension 1, may hold values from -4 to 4
- new_kv: bfloat16 [16, 32, 2, 1024], P('section', 'rep', None, 'tp'), parts along dimension 1, may hold values from -4 to 4
- stream_in: bfloat16 [32, 16384], P('rep', 'tp'), parts along dimension 0, may hold values from -4 to 4
- page_map: int32 [512], P('rep'), parts along dimension 0, may hold values from 0 to 127, each once
- page_counts: int32 [32], P('rep'), parts along dimension 0, may hold values from 1 to 32, 128 in all
- last_fill: int32 [32], P('rep'), parts along dimension 0, may hold values from 1 to 16
Outputs:
- attended: bfloat16 [16, 32, 16384], P('section', 'rep', 'tp'), parts along dimension 1
There are 4 independent parts, one for each index of `rep`. A program takes and returns all parts, laid end to end along the dimension named above; each array names one. Nothing has to cross between parts.
Inputs may be any that keep to these rules, and one draw needn't show every extreme that they name: Request r owns the pool pages page_map[o_r], ..., page_map[o_r + page_counts[r] - 1], o_r being the sum of page_counts over earlier requests; every pool page belongs to exactly one request. `page_counts`: the counts sum to 128.
All inputs are finite; a program needn't handle non-finite values.
Results may differ from a plain program's by a relative error of at most 0.019.
Values may be sent and summed in bfloat16 or wider, within the bound.
A program may use at most 64 MiB of HBM per device.

v0:
```python
import math

import jax
import jax.numpy as jnp
from jax import lax
from jax.sharding import PartitionSpec as P

MAXP = 32
MICRO = 4


epsilon = 1e-05


def shifted(block, axis, distance):
    devices = range(lax.axis_size(axis))
    route = [(i - distance, i) for i in devices if i - distance in devices]
    return lax.ppermute(block, axis, route)


def build_tables(page_map, page_counts, last_fill, page_len):
    offsets = jnp.cumsum(page_counts) - page_counts
    column = jnp.arange(MAXP, dtype=jnp.int32)
    position = offsets[:, None] + jnp.minimum(column[None, :], page_counts[:, None] - 1)
    page_ids = page_map[position]
    length = (page_counts - 1) * page_len + last_fill
    token_pos = jnp.arange(MAXP * page_len, dtype=jnp.int32)
    return (page_ids, token_pos[None, :] < length[:, None])


def normed(stream, head_dim):
    values = stream.astype(jnp.float32)
    shaped = values.reshape(values.shape[0], -1, head_dim)
    scaled = shaped * lax.rsqrt(jnp.mean(shaped * shaped, axis=-1, keepdims=True) + epsilon)
    return scaled.reshape(values.shape)


def attend_block(
    current, row_start, row_count, queries_row, new_entries, resident, page_ids, live, head_dim
):
    query_arg = lax.dynamic_slice_in_dim(queries_row, row_start, row_count, 0)
    new_entry = lax.dynamic_slice_in_dim(new_entries, row_start, row_count, 0)
    page_rows = lax.dynamic_slice_in_dim(page_ids, row_start, row_count, 0)
    visible = lax.dynamic_slice_in_dim(live, row_start, row_count, 0)
    gathered = resident[page_rows]
    key_rows = gathered[:, :, 0].reshape(row_count, -1, head_dim)
    value_rows = gathered[:, :, 1].reshape(row_count, -1, head_dim)
    query_rows = (query_arg.astype(jnp.float32) + normed(current, head_dim)).astype(jnp.bfloat16)
    query_rows = query_rows.reshape(row_count, -1, head_dim)
    scale = 1.0 / math.sqrt(head_dim)
    scores = (
        jnp.einsum("rgd,rtd->rgt", query_rows, key_rows, preferred_element_type=jnp.float32) * scale
    )
    own_score = (
        jnp.einsum("rgd,rd->rg", query_rows, new_entry[:, 0], preferred_element_type=jnp.float32)
        * scale
    )
    live_mask = visible[:, None, :]
    highest = jnp.maximum(jnp.max(jnp.where(live_mask, scores, -1e30), axis=-1), own_score)
    weights = jnp.where(live_mask, jnp.exp(scores - highest[..., None]), 0.0)
    own_weight = jnp.exp(own_score - highest)
    denominator = jnp.sum(weights, axis=-1) + own_weight
    weights = (weights / denominator[..., None]).astype(jnp.bfloat16)
    own_weight = (own_weight / denominator).astype(jnp.bfloat16)
    mixture = jnp.einsum("rgt,rtd->rgd", weights, value_rows, preferred_element_type=jnp.float32)
    mixture = (
        mixture
        + own_weight.astype(jnp.float32)[..., None]
        * new_entry[:, 1].astype(jnp.float32)[:, None, :]
    )
    attended = mixture.astype(jnp.bfloat16).reshape(row_count, -1)
    passed = (current.astype(jnp.float32) + attended.astype(jnp.float32)).astype(jnp.bfloat16)
    return (attended, passed)


def shards(pool, queries, new_kv, stream_in, page_map, page_counts, last_fill):
    head_dim = new_kv.shape[3]
    page_len = pool.shape[3] // head_dim
    section_count = lax.axis_size("section")
    arrived = lax.all_to_all(pool, ("section", "tp"), split_axis=1, concat_axis=0, tiled=True)
    resident = arrived.reshape(arrived.shape[0], 2, arrived.shape[3])
    page_ids, live = build_tables(page_map, page_counts, last_fill, page_len)
    queries_row = queries[0]
    new_entries = new_kv[0]
    total_rows = stream_in.shape[0]
    batch_rows = total_rows // MICRO
    my_section = lax.axis_index("section")

    def run_rows(current, row_start, row_count):
        return attend_block(
            current,
            row_start,
            row_count,
            queries_row,
            new_entries,
            resident,
            page_ids,
            live,
            head_dim,
        )

    def skipped(current):
        return (jnp.zeros_like(current), jnp.zeros_like(current))

    def compute(current):
        pieces = [
            run_rows(
                current[batch_idx * batch_rows : (batch_idx + 1) * batch_rows],
                batch_idx * batch_rows,
                batch_rows,
            )
            for batch_idx in range(MICRO)
        ]
        return (
            jnp.concatenate([piece[0] for piece in pieces], 0),
            jnp.concatenate([piece[1] for piece in pieces], 0),
        )

    def advance(tick_idx, loop_state):
        current, result = loop_state
        attended, passed = lax.cond(tick_idx == my_section, compute, skipped, current)
        result = jnp.where(tick_idx == my_section, attended, result)
        current = shifted(passed, "section", 1)
        return (current, result)

    finished, result = lax.fori_loop(
        0, section_count, advance, (stream_in, jnp.zeros_like(stream_in))
    )
    return result[None]


def solution(mesh):
    in_specs = (
        P(("rep", "section", "tp"), None, None, None),
        P("section", "rep", "tp"),
        P("section", "rep", None, "tp"),
        P("rep", "tp"),
        P("rep"),
        P("rep"),
        P("rep"),
    )
    out_specs = P("section", "rep", "tp")
    return jax.shard_map(shards, mesh=mesh, in_specs=in_specs, out_specs=out_specs, check_vma=False)
```

profile of v0, /device:TPU:494, one launch (start us, length us, event | category | flops | bytes accessed | tf_op | source)
XLA Modules:
  0.0 481.7 jit_solution(2113022102204958521)
XLA Ops:
  0.0 13.4 %all-to-all-start = ((bf16[1,128,2,2048]{3,2,0,1:T(2,128)(2,1)}), bf16[1,128,2,2048]{3,2,0,1:T(2,128)(2,1)S(1)}, u32[]{:S(2)}, u32[]{:S(2)}) async-start(bf16[1,128,2,2048]{3,2,0,1:T(2,128)(2,1)} %bitcast.165), calls=%async_computation | async-start | bytes 2097152 | tf_op jit(solution)/shard_map/all_to_all | solution.py:80
  13.5 0.6 copy-done.6
  14.1 0.2 reduce-window.9
  14.3 0.5 copy-done.5
  15.0 1.9 gather_fusion.4
  16.9 0.6 copy-done.4
  17.5 45.3 %all-to-all-done = bf16[1,128,2,2048]{3,2,0,1:T(2,128)(2,1)S(1)} async-done(((bf16[1,128,2,2048]{3,2,0,1:T(2,128)(2,1)}), bf16[1,128,2,2048]{3,2,0,1:T(2,128)(2,1)S(1)}, u32[]{:S(2)}, u32[]{:S(2)}) %all-to-all-start) | async-done | bytes 1048608 | tf_op jit(solution)/shard_map/all_to_all | solution.py:80
  62.9 418.2 %while.16 = (s32[]{:T(128)}, bf16[8,2048]{1,0:T(8,128)(2,1)S(1)}, bf16[8,2048]{1,0:T(8,128)(2,1)S(1)}, s32[]{:T(128)}, bf16[8,2048]{1,0:T(8,128)(2,1)S(1)}, /*in...) while((s32[]{:T(128)}, bf16[8,2048]{1,0:T(8,128)(2,1)S(1)}, ...), condition=%wide.region_16.17_spmd.clone, body=%wide.region_1.16_spmd.clone.sunk | while | flops 34794244 | bytes 16588566 | solution.py:126
  62.9 1.3 collective-permute-start
  64.3 5.7 %collective-permute-done = bf16[8,2048]{1,0:T(8,128)(2,1)S(1)} collective-permute-done((bf16[8,2048]{1,0:T(8,128)(2,1)S(1)}, bf16[8,2048]{1,0:T(8,128)(2,1)S(1)}, u32[]{:S(2)}, u32[]{:S(2)}) %collective-permute-start) | collective-permute-done | bytes 32800 | tf_op jit(solution)/shard_map/while/body/eval_jaxpr/ppermute | solution.py:18
  69.9 1.3 collective-permute-start
  71.3 4.5 collective-permute-done
  75.8 1.3 collective-permute-start
  77.1 4.5 collective-permute-done
  81.6 1.3 collective-permute-start
  83.0 4.5 collective-permute-done
  87.5 1.3 collective-permute-start
  88.8 5.1 %collective-permute-done = bf16[8,2048]{1,0:T(8,128)(2,1)S(1)} collective-permute-done((bf16[8,2048]{1,0:T(8,128)(2,1)S(1)}, bf16[8,2048]{1,0:T(8,128)(2,1)S(1)}, u32[]{:S(2)}, u32[]{:S(2)}) %collective-permute-start) | collective-permute-done | bytes 32800 | tf_op jit(solution)/shard_map/while/body/eval_jaxpr/ppermute | solution.py:18
  93.9 1.3 collective-permute-start
  95.3 5.6 %collective-permute-done = bf16[8,2048]{1,0:T(8,128)(2,1)S(1)} collective-permute-done((bf16[8,2048]{1,0:T(8,128)(2,1)S(1)}, bf16[8,2048]{1,0:T(8,128)(2,1)S(1)}, u32[]{:S(2)}, u32[]{:S(2)}) %collective-permute-start) | collective-permute-done | bytes 32800 | tf_op jit(solution)/shard_map/while/body/eval_jaxpr/ppermute | solution.py:18
  100.9 1.3 collective-permute-start
  102.2 5.5 %collective-permute-done = bf16[8,2048]{1,0:T(8,128)(2,1)S(1)} collective-permute-done((bf16[8,2048]{1,0:T(8,128)(2,1)S(1)}, bf16[8,2048]{1,0:T(8,128)(2,1)S(1)}, u32[]{:S(2)}, u32[]{:S(2)}) %collective-permute-start) | collective-permute-done | bytes 32800 | tf_op jit(solution)/shard_map/while/body/eval_jaxpr/ppermute | solution.py:18
  107.8 1.3 collective-permute-start
  109.1 5.7 %collective-permute-done = bf16[8,2048]{1,0:T(8,128)(2,1)S(1)} collective-permute-done((bf16[8,2048]{1,0:T(8,128)(2,1)S(1)}, bf16[8,2048]{1,0:T(8,128)(2,1)S(1)}, u32[]{:S(2)}, u32[]{:S(2)}) %collective-permute-start) | collective-permute-done | bytes 32800 | tf_op jit(solution)/shard_map/while/body/eval_jaxpr/ppermute | solution.py:18
  114.8 1.3 collective-permute-start
  116.2 5.7 %collective-permute-done = bf16[8,2048]{1,0:T(8,128)(2,1)S(1)} collective-permute-done((bf16[8,2048]{1,0:T(8,128)(2,1)S(1)}, bf16[8,2048]{1,0:T(8,128)(2,1)S(1)}, u32[]{:S(2)}, u32[]{:S(2)}) %collective-permute-start) | collective-permute-done | bytes 32800 | tf_op jit(solution)/shard_map/while/body/eval_jaxpr/ppermute | solution.py:18
  121.9 1.3 collective-permute-start
  123.2 5.8 %collective-permute-done = bf16[8,2048]{1,0:T(8,128)(2,1)S(1)} collective-permute-done((bf16[8,2048]{1,0:T(8,128)(2,1)S(1)}, bf16[8,2048]{1,0:T(8,128)(2,1)S(1)}, u32[]{:S(2)}, u32[]{:S(2)}) %collective-permute-start) | collective-permute-done | bytes 32800 | tf_op jit(solution)/shard_map/while/body/eval_jaxpr/ppermute | solution.py:18
  129.0 1.3 collective-permute-start
  130.4 5.9 %collective-permute-done = bf16[8,2048]{1,0:T(8,128)(2,1)S(1)} collective-permute-done((bf16[8,2048]{1,0:T(8,128)(2,1)S(1)}, bf16[8,2048]{1,0:T(8,128)(2,1)S(1)}, u32[]{:S(2)}, u32[]{:S(2)}) %collective-permute-start) | collective-permute-done | bytes 32800 | tf_op jit(solution)/shard_map/while/body/eval_jaxpr/ppermute | solution.py:18
  136.3 1.3 collective-permute-start
  137.6 5.4 %collective-permute-done = bf16[8,2048]{1,0:T(8,128)(2,1)S(1)} collective-permute-done((bf16[8,2048]{1,0:T(8,128)(2,1)S(1)}, bf16[8,2048]{1,0:T(8,128)(2,1)S(1)}, u32[]{:S(2)}, u32[]{:S(2)}) %collective-permute-start) | collective-permute-done | bytes 32800 | tf_op jit(solution)/shard_map/while/body/eval_jaxpr/ppermute | solution.py:18
  143.1 1.3 collective-permute-start
  144.4 5.7 %collective-permute-done = bf16[8,2048]{1,0:T(8,128)(2,1)S(1)} collective-permute-done((bf16[8,2048]{1,0:T(8,128)(2,1)S(1)}, bf16[8,2048]{1,0:T(8,128)(2,1)S(1)}, u32[]{:S(2)}, u32[]{:S(2)}) %collective-permute-start) | collective-permute-done | bytes 32800 | tf_op jit(solution)/shard_map/while/body/eval_jaxpr/ppermute | solution.py:18
  150.1 1.3 collective-permute-start
  151.4 5.7 %collective-permute-done = bf16[8,2048]{1,0:T(8,128)(2,1)S(1)} collective-permute-done((bf16[8,2048]{1,0:T(8,128)(2,1)S(1)}, bf16[8,2048]{1,0:T(8,128)(2,1)S(1)}, u32[]{:S(2)}, u32[]{:S(2)}) %collective-permute-start) | collective-permute-done | bytes 32800 | tf_op jit(solution)/shard_map/while/body/eval_jaxpr/ppermute | solution.py:18
  157.2 1.3 collective-permute-start
  158.5 295.8 %collective-permute-done = bf16[8,2048]{1,0:T(8,128)(2,1)S(1)} collective-permute-done((bf16[8,2048]{1,0:T(8,128)(2,1)S(1)}, bf16[8,2048]{1,0:T(8,128)(2,1)S(1)}, u32[]{:S(2)}, u32[]{:S(2)}) %collective-permute-start) | collective-permute-done | bytes 32800 | tf_op jit(solution)/shard_map/while/body/eval_jaxpr/ppermute | solution.py:18
  454.3 21.0 %conditional.3 = (bf16[8,2048]{1,0:T(8,128)(2,1)S(1)}, bf16[8,2048]{1,0:T(8,128)(2,1)S(1)}) conditional(s32[]{:T(128)} %convert_element_type.249, () %tuple.82, (s32[8,512]{1,0:T(8,128)S(1)}, bf16[8,2048]{1,0:T(8,128)(2,1)S(1)}, bf16[8,2048]{1,0:T(8,128)(2,1)S(1)}, s32[8,32]{1,0:T(8,128)S(1)}, bf16[128,2,2048]{2,1,0:T(2,128)(2,1)S(1)}, ...), branch_computations={%region_2.2_spmd, %region_3.15_spmd} | conditional | flops 34761472 | bytes 16342576 | solution.py:121
  455.2 1.6 gather_fusion.1
  456.8 2.3 slice_reduce_fusion.5
  459.3 0.3 select_reduce_fusion.2
  459.8 1.6 gather_fusion
  461.4 2.3 slice_reduce_fusion.7
  463.8 0.3 select_reduce_fusion.3
  464.2 0.2 fusion.10
  464.4 0.1 squeeze.12
  464.5 0.2 fusion.9
  464.8 0.1 squeeze.37
  464.9 0.2 fusion.8
  465.2 1.6 gather_fusion.3
  466.8 2.3 slice_reduce_fusion.1
  469.2 0.3 select_reduce_fusion
  469.7 1.6 gather_fusion.2
  471.3 2.3 slice_reduce_fusion.3
  473.7 0.3 select_reduce_fusion.1
  474.1 0.2 fusion.12
  474.3 0.1 squeeze.40
  474.5 0.2 fusion.7
  474.7 0.1 squeeze.43
  474.8 0.2 fusion.6
  475.3 1.3 collective-permute-start
  476.6 4.5 collective-permute-done
  481.1 0.6 copy-done.3
  (143 shorter events, 3.6 us)
Async XLA Ops:
  0.0 14.9 %copy-start = (s32[128]{0:T(128)S(1)}, s32[128]{0:T(128)}, u32[]{:S(2)}) copy-start(s32[128]{0:T(128)} %param.15) | copy-start | bytes 1540
  0.0 62.9 %all-to-all-start = ((bf16[1,128,2,2048]{3,2,0,1:T(2,128)(2,1)}), bf16[1,128,2,2048]{3,2,0,1:T(2,128)(2,1)S(1)}, u32[]{:S(2)}, u32[]{:S(2)}) async-start(bf16[1,128,2,2048]{3,2,0,1:T(2,128)(2,1)} %bitcast.165), calls=%async_computation | async-start | bytes 2097152 | tf_op jit(solution)/shard_map/all_to_all | solution.py:80
  13.4 0.7 copy-start.6
  14.1 0.7 copy-start.5
  14.9 47.9 %copy-start.1 = (bf16[8,2048]{1,0:T(8,128)(2,1)S(1)}, bf16[8,2048]{1,0:T(8,128)(2,1)}, u32[]{:S(2)}) copy-start(bf16[8,2048]{1,0:T(8,128)(2,1)} %param.14) | copy-start | bytes 98308
  14.9 47.9 %copy-start.2 = (bf16[1,8,2048]{2,1,0:T(8,128)(2,1)S(1)}, bf16[1,8,2048]{2,1,0:T(8,128)(2,1)}, u32[]{:S(2)}) copy-start(bf16[1,8,2048]{2,1,0:T(8,128)(2,1)} %param.12) | copy-start | bytes 98308
  16.8 0.7 copy-start.4
  62.9 7.0 %collective-permute-start = (bf16[8,2048]{1,0:T(8,128)(2,1)S(1)}, bf16[8,2048]{1,0:T(8,128)(2,1)S(1)}, u32[]{:S(2)}, u32[]{:S(2)}) collective-permute-start(bf16[8,2048]{1,0:T(8,128)(2,1)S(1)} %get-tuple-element.352), channel_id=1, source_target_pairs={{0,32},{32,64},{64,96},{96,128},{128,160},{160,192},{192,224},{224... | collective-permute-start | bytes 98312 | tf_op jit(solution)/shard_map/while/body/eval_jaxpr/ppermute | solution.py:18
  69.9 5.8 %collective-permute-start = (bf16[8,2048]{1,0:T(8,128)(2,1)S(1)}, bf16[8,2048]{1,0:T(8,128)(2,1)S(1)}, u32[]{:S(2)}, u32[]{:S(2)}) collective-permute-start(bf16[8,2048]{1,0:T(8,128)(2,1)S(1)} %get-tuple-element.352), channel_id=1, source_target_pairs={{0,32},{32,64},{64,96},{96,128},{128,160},{160,192},{192,224},{224... | collective-permute-start | bytes 98312 | tf_op jit(solution)/shard_map/while/body/eval_jaxpr/ppermute | solution.py:18
  75.8 5.8 %collective-permute-start = (bf16[8,2048]{1,0:T(8,128)(2,1)S(1)}, bf16[8,2048]{1,0:T(8,128)(2,1)S(1)}, u32[]{:S(2)}, u32[]{:S(2)}) collective-permute-start(bf16[8,2048]{1,0:T(8,128)(2,1)S(1)} %get-tuple-element.352), channel_id=1, source_target_pairs={{0,32},{32,64},{64,96},{96,128},{128,160},{160,192},{192,224},{224... | collective-permute-start | bytes 98312 | tf_op jit(solution)/shard_map/while/body/eval_jaxpr/ppermute | solution.py:18
  81.6 5.8 %collective-permute-start = (bf16[8,2048]{1,0:T(8,128)(2,1)S(1)}, bf16[8,2048]{1,0:T(8,128)(2,1)S(1)}, u32[]{:S(2)}, u32[]{:S(2)}) collective-permute-start(bf16[8,2048]{1,0:T(8,128)(2,1)S(1)} %get-tuple-element.352), channel_id=1, source_target_pairs={{0,32},{32,64},{64,96},{96,128},{128,160},{160,192},{192,224},{224... | collective-permute-start | bytes 98312 | tf_op jit(solution)/shard_map/while/body/eval_jaxpr/ppermute | solution.py:18
  87.5 6.4 %collective-permute-start = (bf16[8,2048]{1,0:T(8,128)(2,1)S(1)}, bf16[8,2048]{1,0:T(8,128)(2,1)S(1)}, u32[]{:S(2)}, u32[]{:S(2)}) collective-permute-start(bf16[8,2048]{1,0:T(8,128)(2,1)S(1)} %get-tuple-element.352), channel_id=1, source_target_pairs={{0,32},{32,64},{64,96},{96,128},{128,160},{160,192},{192,224},{224... | collective-permute-start | bytes 98312 | tf_op jit(solution)/shard_map/while/body/eval_jaxpr/ppermute | solution.py:18
  93.9 6.9 %collective-permute-start = (bf16[8,2048]{1,0:T(8,128)(2,1)S(1)}, bf16[8,2048]{1,0:T(8,128)(2,1)S(1)}, u32[]{:S(2)}, u32[]{:S(2)}) collective-permute-start(bf16[8,2048]{1,0:T(8,128)(2,1)S(1)} %get-tuple-element.352), channel_id=1, source_target_pairs={{0,32},{32,64},{64,96},{96,128},{128,160},{160,192},{192,224},{224... | collective-permute-start | bytes 98312 | tf_op jit(solution)/shard_map/while/body/eval_jaxpr/ppermute | solution.py:18
  100.9 6.9 %collective-permute-start = (bf16[8,2048]{1,0:T(8,128)(2,1)S(1)}, bf16[8,2048]{1,0:T(8,128)(2,1)S(1)}, u32[]{:S(2)}, u32[]{:S(2)}) collective-permute-start(bf16[8,2048]{1,0:T(8,128)(2,1)S(1)} %get-tuple-element.352), channel_id=1, source_target_pairs={{0,32},{32,64},{64,96},{96,128},{128,160},{160,192},{192,224},{224... | collective-permute-start | bytes 98312 | tf_op jit(solution)/shard_map/while/body/eval_jaxpr/ppermute | solution.py:18
  107.8 7.0 %collective-permute-start = (bf16[8,2048]{1,0:T(8,128)(2,1)S(1)}, bf16[8,2048]{1,0:T(8,128)(2,1)S(1)}, u32[]{:S(2)}, u32[]{:S(2)}) collective-permute-start(bf16[8,2048]{1,0:T(8,128)(2,1)S(1)} %get-tuple-element.352), channel_id=1, source_target_pairs={{0,32},{32,64},{64,96},{96,128},{128,160},{160,192},{192,224},{224... | collective-permute-start | bytes 98312 | tf_op jit(solution)/shard_map/while/body/eval_jaxpr/ppermute | solution.py:18
  114.8 7.0 %collective-permute-start = (bf16[8,2048]{1,0:T(8,128)(2,1)S(1)}, bf16[8,2048]{1,0:T(8,128)(2,1)S(1)}, u32[]{:S(2)}, u32[]{:S(2)}) collective-permute-start(bf16[8,2048]{1,0:T(8,128)(2,1)S(1)} %get-tuple-element.352), channel_id=1, source_target_pairs={{0,32},{32,64},{64,96},{96,128},{128,160},{160,192},{192,224},{224... | collective-permute-start | bytes 98312 | tf_op jit(solution)/shard_map/while/body/eval_jaxpr/ppermute | solution.py:18
  121.9 7.1 %collective-permute-start = (bf16[8,2048]{1,0:T(8,128)(2,1)S(1)}, bf16[8,2048]{1,0:T(8,128)(2,1)S(1)}, u32[]{:S(2)}, u32[]{:S(2)}) collective-permute-start(bf16[8,2048]{1,0:T(8,128)(2,1)S(1)} %get-tuple-element.352), channel_id=1, source_target_pairs={{0,32},{32,64},{64,96},{96,128},{128,160},{160,192},{192,224},{224... | collective-permute-start | bytes 98312 | tf_op jit(solution)/shard_map/while/body/eval_jaxpr/ppermute | solution.py:18
  129.0 7.2 %collective-permute-start = (bf16[8,2048]{1,0:T(8,128)(2,1)S(1)}, bf16[8,2048]{1,0:T(8,128)(2,1)S(1)}, u32[]{:S(2)}, u32[]{:S(2)}) collective-permute-start(bf16[8,2048]{1,0:T(8,128)(2,1)S(1)} %get-tuple-element.352), channel_id=1, source_target_pairs={{0,32},{32,64},{64,96},{96,128},{128,160},{160,192},{192,224},{224... | collective-permute-start | bytes 98312 | tf_op jit(solution)/shard_map/while/body/eval_jaxpr/ppermute | solution.py:18
  136.3 6.7 %collective-permute-start = (bf16[8,2048]{1,0:T(8,128)(2,1)S(1)}, bf16[8,2048]{1,0:T(8,128)(2,1)S(1)}, u32[]{:S(2)}, u32[]{:S(2)}) collective-permute-start(bf16[8,2048]{1,0:T(8,128)(2,1)S(1)} %get-tuple-element.352), channel_id=1, source_target_pairs={{0,32},{32,64},{64,96},{96,128},{128,160},{160,192},{192,224},{224... | collective-permute-start | bytes 98312 | tf_op jit(solution)/shard_map/while/body/eval_jaxpr/ppermute | solution.py:18
  143.1 7.0 %collective-permute-start = (bf16[8,2048]{1,0:T(8,128)(2,1)S(1)}, bf16[8,2048]{1,0:T(8,128)(2,1)S(1)}, u32[]{:S(2)}, u32[]{:S(2)}) collective-permute-start(bf16[8,2048]{1,0:T(8,128)(2,1)S(1)} %get-tuple-element.352), channel_id=1, source_target_pairs={{0,32},{32,64},{64,96},{96,128},{128,160},{160,192},{192,224},{224... | collective-permute-start | bytes 98312 | tf_op jit(solution)/shard_map/while/body/eval_jaxpr/ppermute | solution.py:18
  150.1 7.0 %collective-permute-start = (bf16[8,2048]{1,0:T(8,128)(2,1)S(1)}, bf16[8,2048]{1,0:T(8,128)(2,1)S(1)}, u32[]{:S(2)}, u32[]{:S(2)}) collective-permute-start(bf16[8,2048]{1,0:T(8,128)(2,1)S(1)} %get-tuple-element.352), channel_id=1, source_target_pairs={{0,32},{32,64},{64,96},{96,128},{128,160},{160,192},{192,224},{224... | collective-permute-start | bytes 98312 | tf_op jit(solution)/shard_map/while/body/eval_jaxpr/ppermute | solution.py:18
  157.2 297.1 %collective-permute-start = (bf16[8,2048]{1,0:T(8,128)(2,1)S(1)}, bf16[8,2048]{1,0:T(8,128)(2,1)S(1)}, u32[]{:S(2)}, u32[]{:S(2)}) collective-permute-start(bf16[8,2048]{1,0:T(8,128)(2,1)S(1)} %get-tuple-element.352), channel_id=1, source_target_pairs={{0,32},{32,64},{64,96},{96,128},{128,160},{160,192},{192,224},{224... | collective-permute-start | bytes 98312 | tf_op jit(solution)/shard_map/while/body/eval_jaxpr/ppermute | solution.py:18
  475.3 5.8 %collective-permute-start = (bf16[8,2048]{1,0:T(8,128)(2,1)S(1)}, bf16[8,2048]{1,0:T(8,128)(2,1)S(1)}, u32[]{:S(2)}, u32[]{:S(2)}) collective-permute-start(bf16[8,2048]{1,0:T(8,128)(2,1)S(1)} %get-tuple-element.352), channel_id=1, source_target_pairs={{0,32},{32,64},{64,96},{96,128},{128,160},{160,192},{192,224},{224... | collective-permute-start | bytes 98312 | tf_op jit(solution)/shard_map/while/body/eval_jaxpr/ppermute | solution.py:18
  481.1 0.6 copy-start.3
where the time goes:
time: 482 us
  waiting for transfers between devices  421 us (87%)
  starting transfers between devices  34.1 us (7%)
  local copies, waits for them, and re-layouts  21.8 us (5%)
    ppermute x16, waiting for transfers between devices, shifted(): return lax.ppermute(block, axis, route)  375 us
    all_to_all x1, waiting for transfers between devices, shards(): lax.all_to_all(pool, ('section', 'tp'), split_axis=1, concat_axis=0, tile...  45.3 us
    ppermute x16, starting transfers between devices, shifted(): return lax.ppermute(block, axis, route)  20.7 us
    all_to_all x1, starting transfers between devices, shards(): lax.all_to_all(pool, ('section', 'tp'), split_axis=1, concat_axis=0, tile...  13.4 us
  transfers between devices with their start and end apart: 17, of which 17 were waited for; matrix products, arithmetic and copies ran while one was open for 1% of the time, Pallas kernels for 0%

commit v1 on v0

v1 whole, which is shorter than its diff:
```python
import math

import jax
import jax.numpy as jnp
from jax import lax
from jax.experimental import pallas as pl
from jax.experimental.pallas import tpu as pltpu
from jax.sharding import PartitionSpec as P

HD = 128
PAGE = 16
GROUP = 16
ROWS = 8
EPS = 1e-05
HIDDEN = -1e30
MESH = pl.DeviceIdType.MESH
EXP2_SCALE = math.log2(math.e) / math.sqrt(HD)


def contract_last(a, b):
    return lax.dot_general(a, b, (((1,), (1,)), ((), ())), preferred_element_type=jnp.float32)


def by_group(block):
    wide = block.astype(jnp.float32)
    return jnp.concatenate([wide[:, g * HD : (g + 1) * HD] for g in range(GROUP)], axis=0)


def build_bias(page_map_ref, counts_ref, fill_ref, bias_ref, pages):
    place = lax.broadcasted_iota(jnp.int32, (16, pages), 1)
    row = lax.broadcasted_iota(jnp.int32, (16, pages), 0)
    limit = jnp.zeros((16, pages), jnp.int32)
    first = jnp.int32(0)
    for r in range(ROWS):
        last = first + counts_ref[r] - 1
        here = jnp.where(place < last, PAGE, jnp.where(place == last, fill_ref[r], 0))
        here = jnp.where(place >= first, here, 0)
        limit = jnp.where(row == r, here, limit)
        first = last + 1
    owner = page_map_ref[...] == lax.broadcasted_iota(jnp.int32, (pages, pages), 0)
    limit = contract_last(
        limit.astype(jnp.float32).astype(jnp.bfloat16),
        jnp.where(owner, 1.0, 0.0).astype(jnp.bfloat16),
    ).astype(jnp.bfloat16)
    width = 256
    page_row = lax.broadcasted_iota(jnp.int32, (pages, width), 0)
    token = lax.broadcasted_iota(jnp.int32, (pages, width), 1)
    inside = (lax.broadcasted_iota(jnp.int32, (ROWS, width), 1) % PAGE).astype(jnp.float32)
    for j in range(pages * PAGE // width):
        spread = jnp.where((token + j * width) // PAGE == page_row, 1.0, 0.0).astype(jnp.bfloat16)
        most = jnp.dot(limit, spread, preferred_element_type=jnp.float32)[:ROWS]
        bias_ref[:, j * width : (j + 1) * width] = jnp.where(inside < most, 0.0, HIDDEN)
    own_row = lax.broadcasted_iota(jnp.int32, (ROWS, HD), 0)
    own_column = lax.broadcasted_iota(jnp.int32, (ROWS, HD), 1)
    bias_ref[:, pages * PAGE :] = jnp.where(own_row == own_column, 0.0, HIDDEN)


def parting():
    row = lax.broadcasted_iota(jnp.int32, (256, 256), 0)
    column = lax.broadcasted_iota(jnp.int32, (256, 256), 1)
    source = jnp.where(row < 128, 2 * row, 2 * row - 255)
    return jnp.where(column == source, 1.0, 0.0).astype(jnp.bfloat16)


def attend(stream, queries, keys_ref, values_ref, bias_ref, scores_ref, tokens):
    norm = stream * lax.rsqrt(jnp.mean(stream * stream, axis=1, keepdims=True) + EPS)
    query = (queries + norm).astype(jnp.bfloat16)
    count = GROUP * ROWS
    chunks = [(at, 256) for at in range(0, tokens, 256)] + [(tokens, HD)]
    top = jnp.full((count, HD), HIDDEN, jnp.float32)
    for at, size in chunks:
        part = contract_last(query, keys_ref[at : at + size, :])
        part = part.reshape(GROUP, ROWS, size) + bias_ref[:, at : at + size][None]
        part = part.reshape(count, size)
        scores_ref[:, at : at + size] = part
        for lane in range(0, size, HD):
            top = jnp.maximum(top, part[:, lane : lane + HD])
    top = jnp.max(top, axis=1, keepdims=True) * EXP2_SCALE
    total = jnp.zeros((count, HD), jnp.float32)
    mixed = jnp.zeros((count, HD), jnp.float32)
    for at, size in chunks:
        part = jnp.exp2(scores_ref[:, at : at + size] * EXP2_SCALE - top)
        for lane in range(0, size, HD):
            total = total + part[:, lane : lane + HD]
        mixed = mixed + jnp.dot(
            part.astype(jnp.bfloat16),
            values_ref[at : at + size, :],
            preferred_element_type=jnp.float32,
        )
    attended = (mixed / jnp.sum(total, axis=1, keepdims=True)).astype(jnp.bfloat16)
    return attended, (stream + attended.astype(jnp.float32)).astype(jnp.bfloat16)


def relay(
    sections,
    pages,
    kv_ref,
    queries_ref,
    new_ref,
    stream_ref,
    page_map_ref,
    counts_ref,
    fill_ref,
    out_ref,
    keys_ref,
    values_ref,
    bias_ref,
    scores_ref,
    arrived,
    leaving,
    send_sem,
    recv_sem,
):
    me = lax.axis_index("section")
    after, before = lax.rem(me + 1, sections), lax.rem(me + sections - 1, sections)
    barrier = pltpu.get_barrier_semaphore()
    for neighbour in (before, after):
        pl.semaphore_signal(barrier, inc=1, device_id={"section": neighbour}, device_id_type=MESH)
    pl.semaphore_wait(barrier, 2)
    tokens = pages * PAGE
    build_bias(page_map_ref, counts_ref, fill_ref, bias_ref, pages)
    part = parting()
    for c in range(tokens // 128):
        both = jnp.dot(part, kv_ref[c * 256 : (c + 1) * 256, :], preferred_element_type=jnp.float32)
        keys_ref[c * 128 : (c + 1) * 128, :] = both[:128].astype(jnp.bfloat16)
        values_ref[c * 128 : (c + 1) * 128, :] = both[128:].astype(jnp.bfloat16)
    new = new_ref[...].astype(jnp.float32)
    blank = jnp.zeros((HD - ROWS, HD), jnp.float32)
    keys_ref[tokens:, :] = jnp.concatenate([new[:, :HD], blank], 0).astype(jnp.bfloat16)
    values_ref[tokens:, :] = jnp.concatenate([new[:, HD:], blank], 0).astype(jnp.bfloat16)
    copy = pltpu.make_async_remote_copy(
        src_ref=leaving,
        dst_ref=arrived,
        send_sem=send_sem,
        recv_sem=recv_sem,
        device_id={"section": after},
        device_id_type=MESH,
    )

    @pl.when(me == 0)
    def _():
        arrived[...] = by_group(stream_ref[...]).astype(jnp.bfloat16)

    @pl.when(me > 0)
    def _():
        copy.wait_recv()

    attended, passed = attend(
        arrived[...].astype(jnp.float32),
        by_group(queries_ref[...]),
        keys_ref,
        values_ref,
        bias_ref,
        scores_ref,
        tokens,
    )
    leaving[...] = passed

    @pl.when(me < sections - 1)
    def _():
        copy.start()

    out_ref[...] = attended

    @pl.when(me < sections - 1)
    def _():
        copy.wait_send()


def shards(pool, queries, new_kv, stream_in, page_map, page_counts, last_fill):
    sections = lax.axis_size("section")
    pages = page_map.shape[0]
    tokens = pages * PAGE
    arrived = lax.all_to_all(pool, ("section", "tp"), split_axis=1, concat_axis=0, tiled=True)
    kv = arrived.reshape(pages, 2, PAGE, HD).transpose(0, 2, 1, 3).reshape(pages * 2 * PAGE, HD)
    vmem = pl.BlockSpec(memory_space=pltpu.VMEM)
    smem = pl.BlockSpec(memory_space=pltpu.SMEM)
    out = pl.pallas_call(
        lambda *refs: relay(sections, pages, *refs),
        out_shape=jax.ShapeDtypeStruct((GROUP * ROWS, HD), jnp.bfloat16),
        in_specs=[vmem] * 5 + [smem] * 2,
        out_specs=vmem,
        scratch_shapes=[
            pltpu.VMEM((tokens + HD, HD), jnp.bfloat16),
            pltpu.VMEM((tokens + HD, HD), jnp.bfloat16),
            pltpu.VMEM((ROWS, tokens + HD), jnp.float32),
            pltpu.VMEM((GROUP * ROWS, tokens + HD), jnp.float32),
            pltpu.VMEM((GROUP * ROWS, HD), jnp.bfloat16),
            pltpu.VMEM((GROUP * ROWS, HD), jnp.bfloat16),
            pltpu.SemaphoreType.DMA,
            pltpu.SemaphoreType.DMA,
        ],
        compiler_params=pltpu.CompilerParams(
            collective_id=0, has_side_effects=True, vmem_limit_bytes=32 * 1024 * 1024
        ),
    )(
        kv,
        queries[0],
        new_kv.reshape(ROWS, 2 * HD),
        stream_in,
        page_map.reshape(1, pages),
        page_counts,
        last_fill,
    )
    return out.reshape(GROUP, ROWS, HD).transpose(1, 0, 2).reshape(1, ROWS, GROUP * HD)


def solution(mesh):
    in_specs = (
        P(("rep", "section", "tp"), None, None, None),
        P("section", "rep", "tp"),
        P("section", "rep", None, "tp"),
        P("rep", "tp"),
        P("rep"),
        P("rep"),
        P("rep"),
    )
    out_specs = P("section", "rep", "tp")
    return jax.shard_map(shards, mesh=mesh, in_specs=in_specs, out_specs=out_specs, check_vma=False)
```

time: 482 us -> 132 us (0.27)
  the two profiles are of different devices: /device:TPU:494 before, /device:TPU:488 now
where the time goes in v1:
time: 132 us
  Pallas kernels  64.6 us (49%)
  waiting for transfers between devices  52.3 us (40%)
  starting transfers between devices  13.5 us (10%)
    pallas_call x1, Pallas kernels, shards(): pl.pallas_call(lambda *refs: relay(sections, pages, *refs), out_shape=jax...  64.6 us
    all_to_all x1, waiting for transfers between devices, shards(): lax.all_to_all(pool, ('section', 'tp'), split_axis=1, concat_axis=0, tile...  52.3 us
    all_to_all x1, starting transfers between devices, shards(): lax.all_to_all(pool, ('section', 'tp'), split_axis=1, concat_axis=0, tile...  13.5 us
  transfers between devices with their start and end apart: 1, of which 1 were waited for; matrix products, arithmetic and copies ran while one was open for 0% of the time, Pallas kernels for 0%

profile of v1, /device:TPU:488, one launch (start us, length us, event | category | flops | bytes accessed | tf_op | source)
XLA Modules:
  0.0 131.7 jit_solution(18201924407500162635)
XLA Ops:
  0.0 0.0 copy-start.5
  0.0 0.0 copy-start
  0.0 0.0 copy-start.1
  0.0 13.5 %all-to-all-start = ((bf16[1,128,2,2048]{3,2,0,1:T(2,128)(2,1)}), bf16[1,128,2,2048]{3,2,0,1:T(2,128)(2,1)S(1)}, u32[]{:S(2)}, u32[]{:S(2)}) async-start(bf16[1,128,2,2048]{3,2,0,1:T(2,128)(2,1)} %bitcast.23), calls=%async_computation | async-start | bytes 2097152 | tf_op jit(solution)/shard_map/all_to_all | solution.py:174
  13.5 0.0 copy-done.5
  13.5 52.3 %all-to-all-done = bf16[1,128,2,2048]{3,2,0,1:T(2,128)(2,1)S(1)} async-done(((bf16[1,128,2,2048]{3,2,0,1:T(2,128)(2,1)}), bf16[1,128,2,2048]{3,2,0,1:T(2,128)(2,1)S(1)}, u32[]{:S(2)}, u32[]{:S(2)}) %all-to-all-start) | async-done | bytes 1048608 | tf_op jit(solution)/shard_map/all_to_all | solution.py:174
  65.8 0.0 copy-start.2
  65.8 0.0 copy-start.3
  65.8 0.0 copy-start.4
  65.8 0.0 copy-done
  65.8 0.0 copy-done.1
  65.8 0.6 copy-done.2
  66.5 0.0 copy-done.3
  66.5 0.0 copy-done.4
  66.5 64.6 %shard_map.73 = bf16[128,128]{1,0:T(8,128)(2,1)S(1)} custom-call(bf16[4096,128]{1,0:T(8,128)(2,1)S(1)} %bitcast.18, bf16[8,2048]{1,0:T(8,128)(2,1)S(1)} %bitcast.20, bf16[8,256]{1,0:T(8,128)(2,1)S(1)} %bitcast.21, bf16[8,2048]{1,0:T(8,128)(2,1)S(1)} %copy-done.1, s32[1,128]{1,0:T(1,128)S(1)} %bitcast.22, s32[8]{0:T(128)S(1)} %copy-done.3, s32[8]{0:T(128)S(1)} %copy-done.4), custom_call_target="tpu_custom_call" | custom-call | tf_op jit(solution)/shard_map/pallas_call | solution.py:178
  131.1 0.6 copy.15
  (1 shorter events, 0.0 us)
Async XLA Ops:
  0.0 13.5 %copy-start.5 = (bf16[1,8,2,128]{3,2,1,0:T(2,128)(2,1)S(1)}, bf16[1,8,2,128]{3,2,1,0:T(2,128)(2,1)}, u32[]{:S(2)}) copy-start(bf16[1,8,2,128]{3,2,1,0:T(2,128)(2,1)} %param.9) | copy-start | bytes 12292
  0.0 65.8 %copy-start = (bf16[1,8,2048]{2,1,0:T(8,128)(2,1)S(1)}, bf16[1,8,2048]{2,1,0:T(8,128)(2,1)}, u32[]{:S(2)}) copy-start(bf16[1,8,2048]{2,1,0:T(8,128)(2,1)} %param.8) | copy-start | bytes 98308
  0.0 65.8 %copy-start.1 = (bf16[8,2048]{1,0:T(8,128)(2,1)S(1)}, bf16[8,2048]{1,0:T(8,128)(2,1)}, u32[]{:S(2)}) copy-start(bf16[8,2048]{1,0:T(8,128)(2,1)} %refs_3_.1) | copy-start | bytes 98308
  0.0 65.8 %all-to-all-start = ((bf16[1,128,2,2048]{3,2,0,1:T(2,128)(2,1)}), bf16[1,128,2,2048]{3,2,0,1:T(2,128)(2,1)S(1)}, u32[]{:S(2)}, u32[]{:S(2)}) async-start(bf16[1,128,2,2048]{3,2,0,1:T(2,128)(2,1)} %bitcast.23), calls=%async_computation | async-start | bytes 2097152 | tf_op jit(solution)/shard_map/all_to_all | solution.py:174
  65.8 0.7 copy-start.2
  65.8 0.7 copy-start.3
  65.8 0.7 copy-start.4

commit v2 on v1

--- a/solution.py
+++ b/solution.py
@@ -13,6 +13,11 @@
 ROWS = 8
 EPS = 1e-05
 HIDDEN = -1e30
+SEGMENTS = 4
+FIRST_HOST = 5
+AHEAD = 2
+BUNDLE = 2
+FAR_AFTER = 1
 MESH = pl.DeviceIdType.MESH
 EXP2_SCALE = math.log2(math.e) / math.sqrt(HD)
 
@@ -91,10 +96,15 @@
     return attended, (stream + attended.astype(jnp.float32)).astype(jnp.bfloat16)
 
 
-def relay(
+def host_of(sections, segments, tp, segment):
+    apart = sections // (2 * segments)
+    return lax.rem(apart * segment + FIRST_HOST + lax.rem(tp, 2) * (sections // 2), sections)
+
+
+def fused(
     sections,
-    pages,
-    kv_ref,
+    heads,
+    pool_ref,
     queries_ref,
     new_ref,
     stream_ref,
@@ -102,99 +112,264 @@
     counts_ref,
     fill_ref,
     out_ref,
+    row_ref,
+    pages_ref,
     keys_ref,
     values_ref,
     bias_ref,
     scores_ref,
+    asked,
+    asking,
     arrived,
     leaving,
-    send_sem,
-    recv_sem,
+    results,
+    row_send,
+    row_recv,
+    page_send,
+    page_recv,
+    ask_send,
+    ask_recv,
+    stream_send,
+    stream_recv,
+    out_send,
+    out_recv,
+    far_sem,
 ):
-    me = lax.axis_index("section")
-    after, before = lax.rem(me + 1, sections), lax.rem(me + sections - 1, sections)
+    z, tp = lax.axis_index("section"), lax.axis_index("tp")
+    depth = pages_ref.shape[0]
+    segments = sections // depth
+    pages = sections * heads
+    tokens = pages * PAGE
+    count = GROUP * ROWS
+
+    def at_section(other):
+        return {"section": other}
+
+    def push(src, dst, send_sem, recv_sem, other):
+        @pl.when(other == z)
+        def _():
+            pltpu.make_async_copy(src, dst, recv_sem).start()
+
+        @pl.when(other != z)
+        def _():
+            pltpu.make_async_remote_copy(
+                src_ref=src,
+                dst_ref=dst,
+                send_sem=send_sem,
+                recv_sem=recv_sem,
+                device_id=at_section(other),
+                device_id_type=MESH,
+            ).start()
+
+    def wait_bytes(ref, sem):
+        pltpu.make_async_copy(ref, ref, sem).wait()
+
+    segment = jnp.int32(-1)
+    for s in range(segments):
+        segment = jnp.where(host_of(sections, segments, tp, s) == z, s, segment)
+    hosting = segment >= 0
+
+    reach = sections // 4
     barrier = pltpu.get_barrier_semaphore()
-    for neighbour in (before, after):
-        pl.semaphore_signal(barrier, inc=1, device_id={"section": neighbour}, device_id_type=MESH)
-    pl.semaphore_wait(barrier, 2)
-    tokens = pages * PAGE
-    build_bias(page_map_ref, counts_ref, fill_ref, bias_ref, pages)
-    part = parting()
-    for c in range(tokens // 128):
-        both = jnp.dot(part, kv_ref[c * 256 : (c + 1) * 256, :], preferred_element_type=jnp.float32)
-        keys_ref[c * 128 : (c + 1) * 128, :] = both[:128].astype(jnp.bfloat16)
-        values_ref[c * 128 : (c + 1) * 128, :] = both[128:].astype(jnp.bfloat16)
+    for d in range(1, reach + 1):
+        for other in (lax.rem(z + d, sections), lax.rem(z + sections - d, sections)):
+            pl.semaphore_signal(
+                barrier, inc=1, device_id=at_section(other), device_id_type=MESH
+            )
+    for d in range(1, heads):
+        pl.semaphore_signal(
+            barrier, inc=1, device_id={"tp": lax.rem(tp + d, heads)}, device_id_type=MESH
+        )
+    asking[:count, :] = by_group(queries_ref[...]).astype(jnp.bfloat16)
     new = new_ref[...].astype(jnp.float32)
-    blank = jnp.zeros((HD - ROWS, HD), jnp.float32)
-    keys_ref[tokens:, :] = jnp.concatenate([new[:, :HD], blank], 0).astype(jnp.bfloat16)
-    values_ref[tokens:, :] = jnp.concatenate([new[:, HD:], blank], 0).astype(jnp.bfloat16)
-    copy = pltpu.make_async_remote_copy(
-        src_ref=leaving,
-        dst_ref=arrived,
-        send_sem=send_sem,
-        recv_sem=recv_sem,
-        device_id={"section": after},
-        device_id_type=MESH,
-    )
-
-    @pl.when(me == 0)
+    asking[count:, :] = jnp.concatenate([new[:, :HD], new[:, HD:]], 0).astype(jnp.bfloat16)
+    pl.semaphore_wait(barrier, heads - 1 + 2 * reach)
+    for other in (lax.rem(z + reach, sections), lax.rem(z + sections - reach, sections)):
+        pl.semaphore_signal(far_sem, inc=1, device_id=at_section(other), device_id_type=MESH)
+
+    bundles = sections // BUNDLE
+    for b in range(bundles):
+        layers = pl.ds(b * BUNDLE, BUNDLE)
+        for d in range(1, heads):
+            other = lax.rem(tp + d, heads)
+            pltpu.make_async_remote_copy(
+                src_ref=pool_ref.at[layers, other],
+                dst_ref=row_ref.at[layers, tp],
+                send_sem=row_send,
+                recv_sem=row_recv.at[b],
+                device_id={"tp": other},
+                device_id_type=MESH,
+            ).start()
+        pltpu.make_async_copy(
+            pool_ref.at[layers, tp], row_ref.at[layers, tp], row_recv.at[b]
+        ).start()
+
+    def forward(b, near):
+        s = b * BUNDLE // depth
+        host = host_of(sections, segments, tp, s)
+        ahead = lax.rem(host - z + sections, sections)
+        close = jnp.logical_or(ahead <= reach, ahead >= sections - reach)
+
+        @pl.when(close if near else jnp.logical_not(close))
+        def _():
+            for i in range(BUNDLE):
+                j = (b * BUNDLE + i) % depth
+                push(row_ref.at[s * depth + j], pages_ref.at[j, z], page_send, page_recv.at[j], host)
+
+    for b in range(bundles):
+        wait_bytes(row_ref.at[pl.ds(b * BUNDLE, BUNDLE)], row_recv.at[b])
+        forward(b, True)
+        if b == FAR_AFTER:
+            pl.semaphore_wait(far_sem, 2)
+            push(asking, asked.at[lax.rem(z, depth)], ask_send, ask_recv,
+                 host_of(sections, segments, tp, z // depth))
+            for earlier in range(b):
+                forward(earlier, False)
+        if b >= FAR_AFTER:
+            forward(b, False)
+
+    @pl.when(hosting)
     def _():
-        arrived[...] = by_group(stream_ref[...]).astype(jnp.bfloat16)
-
-    @pl.when(me > 0)
+        build_bias(page_map_ref, counts_ref, fill_ref, bias_ref, pages)
+        wait_bytes(asked, ask_recv)
+        part = parting()
+        blank = jnp.zeros((HD - ROWS, HD), jnp.float32)
+
+        def prepare(j):
+            wait_bytes(pages_ref.at[j], page_recv.at[j])
+            for c in range(tokens // 128):
+                per = 256 // (2 * PAGE * heads)
+                mixed = pages_ref[j, c * per : (c + 1) * per].reshape(256, HD)
+                both = jnp.dot(part, mixed, preferred_element_type=jnp.float32)
+                keys_ref[j, c * 128 : (c + 1) * 128, :] = both[:128].astype(jnp.bfloat16)
+                values_ref[j, c * 128 : (c + 1) * 128, :] = both[128:].astype(jnp.bfloat16)
+            new = asked[j, count:, :].astype(jnp.float32)
+            keys_ref[j, tokens:, :] = jnp.concatenate([new[:ROWS], blank], 0).astype(jnp.bfloat16)
+            values_ref[j, tokens:, :] = jnp.concatenate([new[ROWS:], blank], 0).astype(jnp.bfloat16)
+
+        def run(j):
+            attended, passed = attend(
+                arrived[...].astype(jnp.float32),
+                asked[j, :count, :].astype(jnp.float32),
+                keys_ref.at[j],
+                values_ref.at[j],
+                bias_ref,
+                scores_ref,
+                tokens,
+            )
+            results[j] = attended
+            push(results.at[j], out_ref, out_send, out_recv, segment * depth + j)
+            return passed
+
+        for j in range(AHEAD):
+            prepare(j)
+
+        onward = pltpu.make_async_remote_copy(
+            src_ref=leaving,
+            dst_ref=arrived,
+            send_sem=stream_send,
+            recv_sem=stream_recv,
+            device_id=at_section(host_of(sections, segments, tp, lax.rem(segment + 1, segments))),
+            device_id_type=MESH,
+        )
+
+        @pl.when(segment == 0)
+        def _():
+            arrived[...] = by_group(stream_ref[...]).astype(jnp.bfloat16)
+
+        @pl.when(segment > 0)
+        def _():
+            onward.wait_recv()
+
+        for j in range(depth):
+            if j >= AHEAD:
+                prepare(j)
+            passed = run(j)
+            if j < depth - 1:
+                arrived[...] = passed
+            else:
+                leaving[...] = passed
+
+        @pl.when(segment < segments - 1)
+        def _():
+            onward.start()
+
+    wait_bytes(out_ref, out_recv)
+    sent = row_ref.at[:, pl.ds(0, heads - 1)]
+    wait_bytes(sent, row_send)
+
+    @pl.when(host_of(sections, segments, tp, z // depth) != z)
     def _():
-        copy.wait_recv()
-
-    attended, passed = attend(
-        arrived[...].astype(jnp.float32),
-        by_group(queries_ref[...]),
-        keys_ref,
-        values_ref,
-        bias_ref,
-        scores_ref,
-        tokens,
-    )
-    leaving[...] = passed
-
-    @pl.when(me < sections - 1)
+        wait_bytes(asking, ask_send)
+
+    @pl.when(hosting)
     def _():
-        copy.start()
-
-    out_ref[...] = attended
-
-    @pl.when(me < sections - 1)
+        wait_bytes(row_ref.at[pl.ds(0, sections - depth)], page_send)
+        at_home = z // depth == segment
+
+        @pl.when(at_home)
+        def _():
+            wait_bytes(results.at[pl.ds(0, depth - 1)], out_send)
+
+        @pl.when(jnp.logical_not(at_home))
+        def _():
+            wait_bytes(results, out_send)
+
+        @pl.when(segment < segments - 1)
+        def _():
+            wait_bytes(leaving, stream_send)
+
+    @pl.when(jnp.logical_not(hosting))
     def _():
-        copy.wait_send()
+        wait_bytes(row_ref, page_send)
 
 
 def shards(pool, queries, new_kv, stream_in, page_map, page_counts, last_fill):
-    sections = lax.axis_size("section")
+    sections, heads = lax.axis_size("section"), lax.axis_size("tp")
     pages = page_map.shape[0]
     tokens = pages * PAGE
-    arrived = lax.all_to_all(pool, ("section", "tp"), split_axis=1, concat_axis=0, tiled=True)
-    kv = arrived.reshape(pages, 2, PAGE, HD).transpose(0, 2, 1, 3).reshape(pages * 2 * PAGE, HD)
+    depth = max(2, sections // SEGMENTS)
+    count = GROUP * ROWS
+    slots = pool.reshape(sections, heads, 2, PAGE, HD).transpose(0, 1, 3, 2, 4)
+    slots = slots.reshape(sections, heads, 2 * PAGE, HD)
     vmem = pl.BlockSpec(memory_space=pltpu.VMEM)
     smem = pl.BlockSpec(memory_space=pltpu.SMEM)
+    dma = pltpu.SemaphoreType.DMA
+    half = jnp.bfloat16
     out = pl.pallas_call(
-        lambda *refs: relay(sections, pages, *refs),
-        out_shape=jax.ShapeDtypeStruct((GROUP * ROWS, HD), jnp.bfloat16),
-        in_specs=[vmem] * 5 + [smem] * 2,
+        lambda *refs: fused(sections, heads, *refs),
+        out_shape=jax.ShapeDtypeStruct((count, HD), half),
+        in_specs=[pl.BlockSpec(memory_space=pl.ANY)] + [vmem] * 4 + [smem] * 2,
         out_specs=vmem,
         scratch_shapes=[
-            pltpu.VMEM((tokens + HD, HD), jnp.bfloat16),
-            pltpu.VMEM((tokens + HD, HD), jnp.bfloat16),
+            pltpu.VMEM((sections, heads, 2 * PAGE, HD), half),
+            pltpu.VMEM((depth, sections, heads, 2 * PAGE, HD), half),
+            pltpu.VMEM((depth, tokens + HD, HD), half),
+            pltpu.VMEM((depth, tokens + HD, HD), half),
             pltpu.VMEM((ROWS, tokens + HD), jnp.float32),
-            pltpu.VMEM((GROUP * ROWS, tokens + HD), jnp.float32),
-            pltpu.VMEM((GROUP * ROWS, HD), jnp.bfloat16),
-            pltpu.VMEM((GROUP * ROWS, HD), jnp.bfloat16),
-            pltpu.SemaphoreType.DMA,
-            pltpu.SemaphoreType.DMA,
+            pltpu.VMEM((count, tokens + HD), jnp.float32),
+            pltpu.VMEM((depth, count + 2 * ROWS, HD), half),
+            pltpu.VMEM((count + 2 * ROWS, HD), half),
+            pltpu.VMEM((count, HD), half),
+            pltpu.VMEM((count, HD), half),
+            pltpu.VMEM((depth, count, HD), half),
+            dma,
+            dma((sections // BUNDLE,)),
+            dma,
+            dma((depth,)),
+            dma,
+            dma,
+            dma,
+            dma,
+            dma,
+            dma,
+            pltpu.SemaphoreType.REGULAR,
         ],
         compiler_params=pltpu.CompilerParams(
             collective_id=0, has_side_effects=True, vmem_limit_bytes=32 * 1024 * 1024
         ),
     )(
-        kv,
+        slots,
         queries[0],
         new_kv.reshape(ROWS, 2 * HD),
         stream_in,

time: 132 us -> 104 us (0.79)
  the two profiles are of different devices: /device:TPU:488 before, /device:TPU:97 now
where the time goes in v2:
time: 104 us
  Pallas kernels  99 us (95%)
  local copies, waits for them, and re-layouts  4.73 us (5%)
    pallas_call x1, Pallas kernels, shards(): pl.pallas_call(lambda *refs: fused(sections, heads, *refs), out_shape=jax...  99 us
    unnamed x16, local copies, waits for them, and re-layouts  4.73 us

profile of v2, /device:TPU:97, one launch (start us, length us, event | category | flops | bytes accessed | tf_op | source)
XLA Modules:
  0.0 103.7 jit_solution(8162682130088011540)
XLA Ops:
  0.0 0.0 copy-start.6
  0.0 0.7 copy-done.6
  0.7 0.0 copy-start.3
  0.7 0.0 copy-start.4
  0.7 0.0 copy-start.5
  0.7 0.6 copy-done.3
  1.3 0.0 copy-done.4
  1.4 0.0 copy-done.5
  1.4 0.0 copy-start
  1.4 1.2 %copy-done = bf16[1,128,2,2048]{3,2,1,0:T(2,128)(2,1)S(1)} copy-done((bf16[1,128,2,2048]{3,2,1,0:T(2,128)(2,1)S(1)}, bf16[1,128,2,2048]{3,2,1,0:T(2,128)(2,1)}, u32[]{:S(2)}) %copy-start) | copy-done | bytes 1048600
  2.6 0.0 copy-start.1
  2.6 0.8 copy-done.1
  3.4 0.0 copy-start.2
  3.4 0.8 copy-done.2
  4.1 99.0 %shard_map.73 = bf16[128,128]{1,0:T(8,128)(2,1)S(1)} custom-call(bf16[16,8,32,128]{3,2,1,0:T(8,128)(2,1)S(1)} %bitcast.17, bf16[8,2048]{1,0:T(8,128)(2,1)S(1)} %bitcast.19, bf16[8,256]{1,0:T(8,128)(2,1)S(1)} %bitcast.20, bf16[8,2048]{1,0:T(8,128)(2,1)S(1)} %copy-done.2, s32[1,128]{1,0:T(1,128)S(1)} %bitcast.21, s32[8]{0:T(128)S(1)} %copy-done.4, s32[8]{0:T(128)S(1)} %copy-done.5), custom_call_target="tpu_custom_call" | custom-call | tf_op jit(solution)/shard_map/pallas_call | solution.py:339
  103.1 0.6 copy.13
  (1 shorter events, 0.0 us)
Async XLA Ops:
  0.0 0.7 copy-start.6
  0.7 0.7 copy-start.3
  0.7 0.7 copy-start.4
  0.7 0.7 copy-start.5
  1.4 1.2 %copy-start = (bf16[1,128,2,2048]{3,2,1,0:T(2,128)(2,1)S(1)}, bf16[1,128,2,2048]{3,2,1,0:T(2,128)(2,1)}, u32[]{:S(2)}) copy-start(bf16[1,128,2,2048]{3,2,1,0:T(2,128)(2,1)} %param.7) | copy-start | bytes 3145732
  2.6 0.8 copy-start.1
  3.4 0.8 copy-start.2

commit v3 on v2

--- a/solution.py
+++ b/solution.py
@@ -14,10 +14,9 @@
 EPS = 1e-05
 HIDDEN = -1e30
 SEGMENTS = 4
-FIRST_HOST = 5
-AHEAD = 2
-BUNDLE = 2
-FAR_AFTER = 1
+FIRST_HOST = 4
+AHEAD = 3
+NEAR_FIRST = 2
 MESH = pl.DeviceIdType.MESH
 EXP2_SCALE = math.log2(math.e) / math.sqrt(HD)
 
@@ -96,9 +95,10 @@
     return attended, (stream + attended.astype(jnp.float32)).astype(jnp.bfloat16)
 
 
-def host_of(sections, segments, tp, segment):
+def host_of(sections, segments, head, segment):
     apart = sections // (2 * segments)
-    return lax.rem(apart * segment + FIRST_HOST + lax.rem(tp, 2) * (sections // 2), sections)
+    start = FIRST_HOST + head // 2 + lax.rem(head, 2) * (sections // 2)
+    return lax.rem(apart * segment + start, sections)
 
 
 def fused(
@@ -112,7 +112,6 @@
     counts_ref,
     fill_ref,
     out_ref,
-    row_ref,
     pages_ref,
     keys_ref,
     values_ref,
@@ -123,8 +122,6 @@
     arrived,
     leaving,
     results,
-    row_send,
-    row_recv,
     page_send,
     page_recv,
     ask_send,
@@ -133,7 +130,9 @@
     stream_recv,
     out_send,
     out_recv,
+    near_sem,
     far_sem,
+    all_sem,
 ):
     z, tp = lax.axis_index("section"), lax.axis_index("tp")
     depth = pages_ref.shape[0]
@@ -170,63 +169,74 @@
     hosting = segment >= 0
 
     reach = sections // 4
+    row_peers = [lax.rem(tp + d, heads) for d in range(1, heads)]
+
+    def tell_row(sem):
+        for other in row_peers:
+            pl.semaphore_signal(sem, inc=1, device_id={"tp": other}, device_id_type=MESH)
+
     barrier = pltpu.get_barrier_semaphore()
     for d in range(1, reach + 1):
         for other in (lax.rem(z + d, sections), lax.rem(z + sections - d, sections)):
             pl.semaphore_signal(
                 barrier, inc=1, device_id=at_section(other), device_id_type=MESH
             )
-    for d in range(1, heads):
-        pl.semaphore_signal(
-            barrier, inc=1, device_id={"tp": lax.rem(tp + d, heads)}, device_id_type=MESH
-        )
+    tell_row(barrier)
     asking[:count, :] = by_group(queries_ref[...]).astype(jnp.bfloat16)
     new = new_ref[...].astype(jnp.float32)
     asking[count:, :] = jnp.concatenate([new[:, :HD], new[:, HD:]], 0).astype(jnp.bfloat16)
     pl.semaphore_wait(barrier, heads - 1 + 2 * reach)
+    tell_row(near_sem)
     for other in (lax.rem(z + reach, sections), lax.rem(z + sections - reach, sections)):
         pl.semaphore_signal(far_sem, inc=1, device_id=at_section(other), device_id_type=MESH)
 
-    bundles = sections // BUNDLE
-    for b in range(bundles):
-        layers = pl.ds(b * BUNDLE, BUNDLE)
-        for d in range(1, heads):
-            other = lax.rem(tp + d, heads)
-            pltpu.make_async_remote_copy(
-                src_ref=pool_ref.at[layers, other],
-                dst_ref=row_ref.at[layers, tp],
-                send_sem=row_send,
-                recv_sem=row_recv.at[b],
-                device_id={"tp": other},
-                device_id_type=MESH,
-            ).start()
-        pltpu.make_async_copy(
-            pool_ref.at[layers, tp], row_ref.at[layers, tp], row_recv.at[b]
-        ).start()
-
-    def forward(b, near):
-        s = b * BUNDLE // depth
-        host = host_of(sections, segments, tp, s)
-        ahead = lax.rem(host - z + sections, sections)
-        close = jnp.logical_or(ahead <= reach, ahead >= sections - reach)
-
-        @pl.when(close if near else jnp.logical_not(close))
-        def _():
-            for i in range(BUNDLE):
-                j = (b * BUNDLE + i) % depth
-                push(row_ref.at[s * depth + j], pages_ref.at[j, z], page_send, page_recv.at[j], host)
-
-    for b in range(bundles):
-        wait_bytes(row_ref.at[pl.ds(b * BUNDLE, BUNDLE)], row_recv.at[b])
-        forward(b, True)
-        if b == FAR_AFTER:
-            pl.semaphore_wait(far_sem, 2)
-            push(asking, asked.at[lax.rem(z, depth)], ask_send, ask_recv,
-                 host_of(sections, segments, tp, z // depth))
-            for earlier in range(b):
-                forward(earlier, False)
-        if b >= FAR_AFTER:
-            forward(b, False)
+    me = z * heads + tp
+
+    def scatter(s, near):
+        def step(i, carry):
+            j = i // heads
+            head = lax.rem(z + tp + i, heads)
+            host = host_of(sections, segments, head, s)
+            ahead = lax.rem(host - z + sections, sections)
+            close = jnp.logical_or(ahead <= reach, ahead >= sections - reach)
+            src = pool_ref.at[s * depth + j, head]
+            dst = pages_ref.at[j, me]
+            mine = jnp.logical_and(host == z, head == tp)
+            wanted = close if near else jnp.logical_not(close)
+            if near is None:
+                wanted = jnp.bool_(True)
+
+            @pl.when(jnp.logical_and(wanted, mine))
+            def _():
+                pltpu.make_async_copy(src, dst, page_recv.at[j]).start()
+
+            @pl.when(jnp.logical_and(wanted, jnp.logical_not(mine)))
+            def _():
+                pltpu.make_async_remote_copy(
+                    src_ref=src,
+                    dst_ref=dst,
+                    send_sem=page_send,
+                    recv_sem=page_recv.at[j],
+                    device_id={"section": host, "tp": head},
+                    device_id_type=MESH,
+                ).start()
+
+            return carry
+
+        lax.fori_loop(0, depth * heads, step, 0)
+
+    pl.semaphore_wait(near_sem, heads - 1)
+    if NEAR_FIRST >= 1:
+        scatter(0, True)
+    pl.semaphore_wait(far_sem, 2)
+    tell_row(all_sem)
+    push(asking, asked.at[lax.rem(z, depth)], ask_send, ask_recv,
+         host_of(sections, segments, tp, z // depth))
+    for s in range(1, NEAR_FIRST):
+        scatter(s, True)
+    pl.semaphore_wait(all_sem, heads - 1)
+    for s in range(segments):
+        scatter(s, False if s < NEAR_FIRST else None)
 
     @pl.when(hosting)
     def _():
@@ -238,7 +248,7 @@
         def prepare(j):
             wait_bytes(pages_ref.at[j], page_recv.at[j])
             for c in range(tokens // 128):
-                per = 256 // (2 * PAGE * heads)
+                per = 256 // (2 * PAGE)
                 mixed = pages_ref[j, c * per : (c + 1) * per].reshape(256, HD)
                 both = jnp.dot(part, mixed, preferred_element_type=jnp.float32)
                 keys_ref[j, c * 128 : (c + 1) * 128, :] = both[:128].astype(jnp.bfloat16)
@@ -295,8 +305,6 @@
             onward.start()
 
     wait_bytes(out_ref, out_recv)
-    sent = row_ref.at[:, pl.ds(0, heads - 1)]
-    wait_bytes(sent, row_send)
 
     @pl.when(host_of(sections, segments, tp, z // depth) != z)
     def _():
@@ -304,7 +312,8 @@
 
     @pl.when(hosting)
     def _():
-        wait_bytes(row_ref.at[pl.ds(0, sections - depth)], page_send)
+        wait_bytes(pool_ref.at[pl.ds(0, sections - 1)], page_send)
+        wait_bytes(pool_ref.at[0, pl.ds(0, heads - depth)], page_send)
         at_home = z // depth == segment
 
         @pl.when(at_home)
@@ -321,14 +330,14 @@
 
     @pl.when(jnp.logical_not(hosting))
     def _():
-        wait_bytes(row_ref, page_send)
+        wait_bytes(pool_ref, page_send)
 
 
 def shards(pool, queries, new_kv, stream_in, page_map, page_counts, last_fill):
     sections, heads = lax.axis_size("section"), lax.axis_size("tp")
     pages = page_map.shape[0]
     tokens = pages * PAGE
-    depth = max(2, sections // SEGMENTS)
+    depth = sections // SEGMENTS
     count = GROUP * ROWS
     slots = pool.reshape(sections, heads, 2, PAGE, HD).transpose(0, 1, 3, 2, 4)
     slots = slots.reshape(sections, heads, 2 * PAGE, HD)
@@ -342,8 +351,7 @@
         in_specs=[pl.BlockSpec(memory_space=pl.ANY)] + [vmem] * 4 + [smem] * 2,
         out_specs=vmem,
         scratch_shapes=[
-            pltpu.VMEM((sections, heads, 2 * PAGE, HD), half),
-            pltpu.VMEM((depth, sections, heads, 2 * PAGE, HD), half),
+            pltpu.VMEM((depth, pages, 2 * PAGE, HD), half),
             pltpu.VMEM((depth, tokens + HD, HD), half),
             pltpu.VMEM((depth, tokens + HD, HD), half),
             pltpu.VMEM((ROWS, tokens + HD), jnp.float32),
@@ -354,8 +362,6 @@
             pltpu.VMEM((count, HD), half),
             pltpu.VMEM((depth, count, HD), half),
             dma,
-            dma((sections // BUNDLE,)),
-            dma,
             dma((depth,)),
             dma,
             dma,
@@ -363,10 +369,12 @@
             dma,
             dma,
             dma,
+            pltpu.SemaphoreType.REGULAR,
+            pltpu.SemaphoreType.REGULAR,
             pltpu.SemaphoreType.REGULAR,
         ],
         compiler_params=pltpu.CompilerParams(
-            collective_id=0, has_side_effects=True, vmem_limit_bytes=32 * 1024 * 1024
+            collective_id=0, has_side_effects=True, vmem_limit_bytes=60 * 1024 * 1024
         ),
     )(
         slots,

time: 104 us -> 88.5 us (0.85)
  the two profiles are of different devices: /device:TPU:97 before, /device:TPU:65 now
where the time goes in v3:
time: 88.5 us; the launch traced here: 88.2 us
  Pallas kernels  85.5 us (97%)
  local copies, waits for them, and re-layouts  2.66 us (3%)
    pallas_call x1, Pallas kernels, shards(): pl.pallas_call(lambda *refs: fused(sections, heads, *refs), out_shape=jax...  85.5 us
    unnamed x4, local copies, waits for them, and re-layouts  2.66 us

profile of v3, /device:TPU:65, one launch (start us, length us, event | category | flops | bytes accessed | tf_op | source)
XLA Modules:
  0.0 88.2 jit_solution(14706283048444827534)
XLA Ops:
  0.0 0.0 copy-start
  0.0 0.7 copy-done
  0.7 0.6 copy.11
  1.3 85.5 %shard_map.73 = bf16[128,128]{1,0:T(8,128)(2,1)} custom-call(bf16[16,8,32,128]{3,2,1,0:T(8,128)(2,1)} %bitcast.17, bf16[8,2048]{1,0:T(8,128)(2,1)} %bitcast.19, bf16[8,256]{1,0:T(8,128)(2,1)} %bitcast.20, bf16[8,2048]{1,0:T(8,128)(2,1)} %refs_3_.1, s32[1,128]{1,0:T(1,128)} %bitcast.21, s32[8]{0:T(128)} %refs_5_.1, s32[8]{0:T(128)} %refs_6_.1), custom_call_target="tpu_custom_call" | custom-call | tf_op jit(solution)/shard_map/pallas_call | solution.py:348
  86.8 1.4 %copy.13 = bf16[1,8,2048]{2,1,0:T(8,128)(2,1)} copy(bf16[1,8,2048]{2,1,0:T(8,128)(2,1)} %bitcast.18) | data formatting | bytes 65536
Async XLA Ops:
  0.0 0.7 copy-start

commit v4 on v3

--- a/solution.py
+++ b/solution.py
@@ -1,3 +1,4 @@
+import functools
 import math
 
 import jax
@@ -13,10 +14,10 @@
 ROWS = 8
 EPS = 1e-05
 HIDDEN = -1e30
-SEGMENTS = 4
-FIRST_HOST = 4
+STARTS = (0, 4, 8, 12, 16)
+FIRST_HOST = 0
 AHEAD = 3
-NEAR_FIRST = 2
+NEAR_FIRST = 1
 MESH = pl.DeviceIdType.MESH
 EXP2_SCALE = math.log2(math.e) / math.sqrt(HD)
 
@@ -95,10 +96,22 @@
     return attended, (stream + attended.astype(jnp.float32)).astype(jnp.bfloat16)
 
 
-def host_of(sections, segments, head, segment):
-    apart = sections // (2 * segments)
-    start = FIRST_HOST + head // 2 + lax.rem(head, 2) * (sections // 2)
-    return lax.rem(apart * segment + start, sections)
+def host_of(sections, heads, head, segment):
+    columns = heads // 2
+    x = lax.rem(head + segment, columns)
+    z = lax.rem((sections // heads) * head + FIRST_HOST + lax.rem(x, 2), sections)
+    return z, 2 * x + lax.rem(segment, 2)
+
+
+def hosted_at(sections, heads, segments, z, tp):
+    columns, stride = heads // 2, sections // heads
+    x = tp // 2
+    rest = lax.rem(z - FIRST_HOST - lax.rem(x, 2) + 2 * sections, sections)
+    head = rest // stride
+    segment = lax.rem(x - head + heads, columns)
+    found = jnp.logical_and(lax.rem(rest, stride) == 0, segment < segments)
+    found = jnp.logical_and(found, lax.rem(segment, 2) == lax.rem(tp, 2))
+    return head, jnp.where(found, segment, -1)
 
 
 def fused(
@@ -112,6 +125,7 @@
     counts_ref,
     fill_ref,
     out_ref,
+    spare_ref,
     pages_ref,
     keys_ref,
     values_ref,
@@ -119,13 +133,16 @@
     scores_ref,
     asked,
     asking,
+    opening,
     arrived,
-    leaving,
     results,
+    spare_send,
+    spare_recv,
     page_send,
     page_recv,
     ask_send,
     ask_recv,
+    open_send,
     stream_send,
     stream_recv,
     out_send,
@@ -135,117 +152,161 @@
     all_sem,
 ):
     z, tp = lax.axis_index("section"), lax.axis_index("tp")
-    depth = pages_ref.shape[0]
-    segments = sections // depth
+    me = z * heads + tp
+    partner = tp + 1 - 2 * lax.rem(tp, 2)
+    segments = len(STARTS) - 1
+    depths = [STARTS[s + 1] - STARTS[s] for s in range(segments)]
     pages = sections * heads
     tokens = pages * PAGE
     count = GROUP * ROWS
 
-    def at_section(other):
-        return {"section": other}
+    def place(other):
+        return {"section": other[0], "tp": other[1]}
+
+    def here(other):
+        return jnp.logical_and(other[0] == z, other[1] == tp)
 
     def push(src, dst, send_sem, recv_sem, other):
-        @pl.when(other == z)
+        @pl.when(here(other))
         def _():
             pltpu.make_async_copy(src, dst, recv_sem).start()
 
-        @pl.when(other != z)
+        @pl.when(jnp.logical_not(here(other)))
         def _():
             pltpu.make_async_remote_copy(
                 src_ref=src,
                 dst_ref=dst,
                 send_sem=send_sem,
                 recv_sem=recv_sem,
-                device_id=at_section(other),
+                device_id=place(other),
                 device_id_type=MESH,
             ).start()
 
     def wait_bytes(ref, sem):
         pltpu.make_async_copy(ref, ref, sem).wait()
 
-    segment = jnp.int32(-1)
+    host = functools.partial(host_of, sections, heads)
+    head, segment = hosted_at(sections, heads, segments, z, tp)
+    other_segment = hosted_at(sections, heads, segments, z, partner)[1]
+    hosting, helping = segment >= 0, other_segment >= 0
+    start, depth = jnp.int32(0), jnp.int32(0)
+    home_start, home_segment = jnp.int32(0), jnp.int32(0)
     for s in range(segments):
-        segment = jnp.where(host_of(sections, segments, tp, s) == z, s, segment)
-    hosting = segment >= 0
+        start = jnp.where(segment == s, STARTS[s], start)
+        depth = jnp.where(segment == s, depths[s], depth)
+        home_start = jnp.where(z >= STARTS[s], STARTS[s], home_start)
+        home_segment = jnp.where(z >= STARTS[s], s, home_segment)
+    home_host, first_host = host(tp, home_segment), host(tp, 0)
+    opens = z == first_host[0]
 
     reach = sections // 4
-    row_peers = [lax.rem(tp + d, heads) for d in range(1, heads)]
 
     def tell_row(sem):
-        for other in row_peers:
-            pl.semaphore_signal(sem, inc=1, device_id={"tp": other}, device_id_type=MESH)
+        for d in range(1, heads):
+            pl.semaphore_signal(
+                sem, inc=1, device_id={"tp": lax.rem(tp + d, heads)}, device_id_type=MESH
+            )
 
     barrier = pltpu.get_barrier_semaphore()
     for d in range(1, reach + 1):
         for other in (lax.rem(z + d, sections), lax.rem(z + sections - d, sections)):
             pl.semaphore_signal(
-                barrier, inc=1, device_id=at_section(other), device_id_type=MESH
+                barrier, inc=1, device_id={"section": other}, device_id_type=MESH
             )
     tell_row(barrier)
+    opening[...] = by_group(stream_ref[...]).astype(jnp.bfloat16)
     asking[:count, :] = by_group(queries_ref[...]).astype(jnp.bfloat16)
     new = new_ref[...].astype(jnp.float32)
     asking[count:, :] = jnp.concatenate([new[:, :HD], new[:, HD:]], 0).astype(jnp.bfloat16)
     pl.semaphore_wait(barrier, heads - 1 + 2 * reach)
     tell_row(near_sem)
     for other in (lax.rem(z + reach, sections), lax.rem(z + sections - reach, sections)):
-        pl.semaphore_signal(far_sem, inc=1, device_id=at_section(other), device_id_type=MESH)
-
-    me = z * heads + tp
-
-    def scatter(s, near):
+        pl.semaphore_signal(far_sem, inc=1, device_id={"section": other}, device_id_type=MESH)
+
+    def spare(s):
+        layers = pl.ds(STARTS[s], depths[s])
+        return pltpu.make_async_remote_copy(
+            src_ref=pool_ref.at[layers],
+            dst_ref=spare_ref.at[layers],
+            send_sem=spare_send.at[s],
+            recv_sem=spare_recv.at[s],
+            device_id={"tp": partner},
+            device_id_type=MESH,
+        )
+
+    @pl.when(hosting)
+    def _():
+        for s in range(segments):
+            spare(s).start()
+            for j in range(depths[s]):
+
+                @pl.when(segment == s)
+                def _():
+                    pltpu.make_async_copy(
+                        pool_ref.at[STARTS[s] + j, head], pages_ref.at[j, me], page_recv.at[j]
+                    ).start()
+
+    def scatter(s, near, source_ref, owner):
         def step(i, carry):
             j = i // heads
-            head = lax.rem(z + tp + i, heads)
-            host = host_of(sections, segments, head, s)
-            ahead = lax.rem(host - z + sections, sections)
-            close = jnp.logical_or(ahead <= reach, ahead >= sections - reach)
-            src = pool_ref.at[s * depth + j, head]
-            dst = pages_ref.at[j, me]
-            mine = jnp.logical_and(host == z, head == tp)
-            wanted = close if near else jnp.logical_not(close)
-            if near is None:
-                wanted = jnp.bool_(True)
-
-            @pl.when(jnp.logical_and(wanted, mine))
-            def _():
-                pltpu.make_async_copy(src, dst, page_recv.at[j]).start()
-
-            @pl.when(jnp.logical_and(wanted, jnp.logical_not(mine)))
+            goal = lax.rem(z + tp + i, heads)
+            other = host(goal, s)
+            wanted = jnp.logical_not(jnp.logical_and(other[0] == z, other[1] == owner))
+            if near is not None:
+                ahead = lax.rem(other[0] - z + sections, sections)
+                close = jnp.logical_or(ahead <= reach, ahead >= sections - reach)
+                wanted = jnp.logical_and(wanted, close if near else jnp.logical_not(close))
+
+            @pl.when(wanted)
             def _():
                 pltpu.make_async_remote_copy(
-                    src_ref=src,
-                    dst_ref=dst,
+                    src_ref=source_ref.at[STARTS[s] + j, goal],
+                    dst_ref=pages_ref.at[j, z * heads + owner],
                     send_sem=page_send,
                     recv_sem=page_recv.at[j],
-                    device_id={"section": host, "tp": head},
+                    device_id=place(other),
                     device_id_type=MESH,
                 ).start()
 
             return carry
 
-        lax.fori_loop(0, depth * heads, step, 0)
+        lax.fori_loop(0, depths[s] * heads, step, 0)
 
     pl.semaphore_wait(near_sem, heads - 1)
-    if NEAR_FIRST >= 1:
-        scatter(0, True)
     pl.semaphore_wait(far_sem, 2)
     tell_row(all_sem)
-    push(asking, asked.at[lax.rem(z, depth)], ask_send, ask_recv,
-         host_of(sections, segments, tp, z // depth))
-    for s in range(1, NEAR_FIRST):
-        scatter(s, True)
+
+    @pl.when(jnp.logical_not(hosting))
+    def _():
+        for s in range(NEAR_FIRST):
+            scatter(s, True, pool_ref, tp)
+
     pl.semaphore_wait(all_sem, heads - 1)
-    for s in range(segments):
-        scatter(s, False if s < NEAR_FIRST else None)
+    push(asking, asked.at[z - home_start], ask_send, ask_recv.at[z - home_start], home_host)
+
+    @pl.when(opens)
+    def _():
+        push(opening, arrived, open_send, stream_recv, first_host)
+
+
+    @pl.when(jnp.logical_not(hosting))
+    def _():
+        for s in range(segments):
+            scatter(s, False if s < NEAR_FIRST else None, pool_ref, tp)
+
+            @pl.when(helping)
+            def _():
+                spare(s).wait_recv()
+                scatter(s, None, spare_ref, partner)
 
     @pl.when(hosting)
     def _():
         build_bias(page_map_ref, counts_ref, fill_ref, bias_ref, pages)
-        wait_bytes(asked, ask_recv)
         part = parting()
         blank = jnp.zeros((HD - ROWS, HD), jnp.float32)
 
         def prepare(j):
+            wait_bytes(asked.at[j], ask_recv.at[j])
             wait_bytes(pages_ref.at[j], page_recv.at[j])
             for c in range(tokens // 128):
                 per = 256 // (2 * PAGE)
@@ -267,77 +328,91 @@
                 scores_ref,
                 tokens,
             )
+            arrived[...] = passed
             results[j] = attended
-            push(results.at[j], out_ref, out_send, out_recv, segment * depth + j)
-            return passed
-
-        for j in range(AHEAD):
-            prepare(j)
+
+        def deliver(j):
+            push(results.at[j], out_ref, out_send.at[j], out_recv, (start + j, head))
+
+        def where_deep(j, act):
+            if j < min(depths):
+                act(j)
+            else:
+                pl.when(depth > j)(functools.partial(act, j))
+
+        for j in range(min(AHEAD, max(depths))):
+            where_deep(j, prepare)
 
         onward = pltpu.make_async_remote_copy(
-            src_ref=leaving,
+            src_ref=arrived,
             dst_ref=arrived,
             send_sem=stream_send,
             recv_sem=stream_recv,
-            device_id=at_section(host_of(sections, segments, tp, lax.rem(segment + 1, segments))),
+            device_id=place(host(head, jnp.minimum(segment + 1, segments - 1))),
             device_id_type=MESH,
         )
 
-        @pl.when(segment == 0)
-        def _():
-            arrived[...] = by_group(stream_ref[...]).astype(jnp.bfloat16)
-
-        @pl.when(segment > 0)
-        def _():
-            onward.wait_recv()
-
-        for j in range(depth):
+        onward.wait_recv()
+
+        def advance(j):
             if j >= AHEAD:
                 prepare(j)
-            passed = run(j)
-            if j < depth - 1:
-                arrived[...] = passed
-            else:
-                leaving[...] = passed
+            run(j)
+
+            @pl.when(jnp.logical_and(j == depth - 1, segment < segments - 1))
+            def _():
+                onward.start()
+
+            deliver(j)
+
+        for j in range(max(depths)):
+            where_deep(j, advance)
+
+        def drain(j):
+            @pl.when(jnp.logical_not(here((start + j, head))))
+            def _():
+                wait_bytes(results.at[j], out_send.at[j])
+
+        for j in range(max(depths)):
+            where_deep(j, drain)
 
         @pl.when(segment < segments - 1)
         def _():
-            onward.start()
+            wait_bytes(arrived, stream_send)
+
+        for s in range(segments):
+            spare(s).wait_send()
 
     wait_bytes(out_ref, out_recv)
 
-    @pl.when(host_of(sections, segments, tp, z // depth) != z)
+    @pl.when(jnp.logical_not(here(home_host)))
     def _():
         wait_bytes(asking, ask_send)
 
-    @pl.when(hosting)
-    def _():
-        wait_bytes(pool_ref.at[pl.ds(0, sections - 1)], page_send)
-        wait_bytes(pool_ref.at[0, pl.ds(0, heads - depth)], page_send)
-        at_home = z // depth == segment
-
-        @pl.when(at_home)
+    @pl.when(jnp.logical_and(opens, jnp.logical_not(here(first_host))))
+    def _():
+        wait_bytes(opening, open_send)
+
+    @pl.when(jnp.logical_not(hosting))
+    def _():
+        wait_bytes(pool_ref, page_send)
+
+        @pl.when(helping)
         def _():
-            wait_bytes(results.at[pl.ds(0, depth - 1)], out_send)
-
-        @pl.when(jnp.logical_not(at_home))
-        def _():
-            wait_bytes(results, out_send)
-
-        @pl.when(segment < segments - 1)
-        def _():
-            wait_bytes(leaving, stream_send)
-
-    @pl.when(jnp.logical_not(hosting))
-    def _():
-        wait_bytes(pool_ref, page_send)
+            wait_bytes(pool_ref.at[pl.ds(0, sections - 1)], page_send)
+            for s in range(segments):
+
+                @pl.when(other_segment == s)
+                def _():
+                    wait_bytes(pool_ref.at[0, pl.ds(0, heads - depths[s])], page_send)
 
 
 def shards(pool, queries, new_kv, stream_in, page_map, page_counts, last_fill):
     sections, heads = lax.axis_size("section"), lax.axis_size("tp")
     pages = page_map.shape[0]
     tokens = pages * PAGE
-    depth = sections // SEGMENTS
+    segments = len(STARTS) - 1
+    depth = max(STARTS[s + 1] - STARTS[s] for s in range(segments))
     count = GROUP * ROWS
     slots = pool.reshape(sections, heads, 2, PAGE, HD).transpose(0, 1, 3, 2, 4)
     slots = slots.reshape(sections, heads, 2 * PAGE, HD)
@@ -351,6 +426,7 @@
         in_specs=[pl.BlockSpec(memory_space=pl.ANY)] + [vmem] * 4 + [smem] * 2,
         out_specs=vmem,
         scratch_shapes=[
+            pltpu.VMEM((sections, heads, 2 * PAGE, HD), half),
             pltpu.VMEM((depth, pages, 2 * PAGE, HD), half),
             pltpu.VMEM((depth, tokens + HD, HD), half),
             pltpu.VMEM((depth, tokens + HD, HD), half),
@@ -361,13 +437,16 @@
             pltpu.VMEM((count, HD), half),
             pltpu.VMEM((count, HD), half),
             pltpu.VMEM((depth, count, HD), half),
+            dma((segments,)),
+            dma((segments,)),
             dma,
             dma((depth,)),
             dma,
-            dma,
-            dma,
-            dma,
-            dma,
+            dma((depth,)),
+            dma,
+            dma,
+            dma,
+            dma((depth,)),
             dma,
             pltpu.SemaphoreType.REGULAR,
             pltpu.SemaphoreType.REGULAR,

time: 88.5 us -> 82.8 us (0.936)
  the two profiles are of different devices: /device:TPU:65 before, /device:TPU:63 now
where the time goes in v4:
time: 82.8 us; the launch traced here: 82.5 us
  Pallas kernels  79.9 us (96%)
  local copies, waits for them, and re-layouts  2.66 us (3%)
    pallas_call x1, Pallas kernels, shards(): pl.pallas_call(lambda *refs: fused(sections, heads, *refs), out_shape=jax...  79.9 us
    unnamed x4, local copies, waits for them, and re-layouts  2.66 us

profile of v4, /device:TPU:63, one launch (start us, length us, event | category | flops | bytes accessed | tf_op | source)
XLA Modules:
  0.0 82.5 jit_solution(16187562947529928662)
XLA Ops:
  0.0 0.0 copy-start
  0.0 0.7 copy-done
  0.7 0.6 copy.11
  1.3 79.9 %shard_map.73 = bf16[128,128]{1,0:T(8,128)(2,1)} custom-call(bf16[16,8,32,128]{3,2,1,0:T(8,128)(2,1)} %bitcast.17, bf16[8,2048]{1,0:T(8,128)(2,1)} %bitcast.19, bf16[8,256]{1,0:T(8,128)(2,1)} %bitcast.20, bf16[8,2048]{1,0:T(8,128)(2,1)} %refs_3_.1, s32[1,128]{1,0:T(1,128)} %bitcast.21, s32[8]{0:T(128)} %refs_5_.1, s32[8]{0:T(128)} %refs_6_.1), custom_call_target="tpu_custom_call" | custom-call | tf_op jit(solution)/shard_map/pallas_call | solution.py:423
  81.2 1.4 %copy.13 = bf16[1,8,2048]{2,1,0:T(8,128)(2,1)} copy(bf16[1,8,2048]{2,1,0:T(8,128)(2,1)} %bitcast.18) | data formatting | bytes 65536
Async XLA Ops:
  0.0 0.7 copy-start

commit v5 on v4

--- a/solution.py
+++ b/solution.py
@@ -15,7 +15,7 @@
 EPS = 1e-05
 HIDDEN = -1e30
 STARTS = (0, 4, 8, 12, 16)
-FIRST_HOST = 0
+FIRST_HOST = 8
 AHEAD = 3
 NEAR_FIRST = 1
 MESH = pl.DeviceIdType.MESH
@@ -216,8 +216,7 @@
     tell_row(barrier)
     opening[...] = by_group(stream_ref[...]).astype(jnp.bfloat16)
     asking[:count, :] = by_group(queries_ref[...]).astype(jnp.bfloat16)
-    new = new_ref[...].astype(jnp.float32)
-    asking[count:, :] = jnp.concatenate([new[:, :HD], new[:, HD:]], 0).astype(jnp.bfloat16)
+    asking[count:, :] = new_ref[...]
     pl.semaphore_wait(barrier, heads - 1 + 2 * reach)
     tell_row(near_sem)
     for other in (lax.rem(z + reach, sections), lax.rem(z + sections - reach, sections)):
@@ -303,7 +302,6 @@
     def _():
         build_bias(page_map_ref, counts_ref, fill_ref, bias_ref, pages)
         part = parting()
-        blank = jnp.zeros((HD - ROWS, HD), jnp.float32)
 
         def prepare(j):
             wait_bytes(asked.at[j], ask_recv.at[j])
@@ -314,9 +312,11 @@
                 both = jnp.dot(part, mixed, preferred_element_type=jnp.float32)
                 keys_ref[j, c * 128 : (c + 1) * 128, :] = both[:128].astype(jnp.bfloat16)
                 values_ref[j, c * 128 : (c + 1) * 128, :] = both[128:].astype(jnp.bfloat16)
-            new = asked[j, count:, :].astype(jnp.float32)
-            keys_ref[j, tokens:, :] = jnp.concatenate([new[:ROWS], blank], 0).astype(jnp.bfloat16)
-            values_ref[j, tokens:, :] = jnp.concatenate([new[ROWS:], blank], 0).astype(jnp.bfloat16)
+            both = jnp.dot(
+                part[:, : 2 * ROWS], asked[j, count:, :], preferred_element_type=jnp.float32
+            )
+            keys_ref[j, tokens:, :] = both[:HD].astype(jnp.bfloat16)
+            values_ref[j, tokens:, :] = both[HD:].astype(jnp.bfloat16)
 
         def run(j):
             attended, passed = attend(
@@ -458,7 +458,7 @@
     )(
         slots,
         queries[0],
-        new_kv.reshape(ROWS, 2 * HD),
+        new_kv.reshape(2 * ROWS, HD),
         stream_in,
         page_map.reshape(1, pages),
         page_counts,

time: 82.8 us -> 81.2 us (0.981)
  local copies, waits for them, and re-layouts: 2.66 us -> 1.38 us
    unnamed x4 -> x1, local copies, waits for them, and re-layouts: 2.66 us -> 1.38 us
where the time goes in v5:
time: 81.2 us; the launch traced here: 81 us
  Pallas kernels  79.6 us (98%)
  local copies, waits for them, and re-layouts  1.38 us (2%)
    pallas_call x1, Pallas kernels, shards(): pl.pallas_call(lambda *refs: fused(sections, heads, *refs), out_shape=jax...  79.6 us

profile of v5, /device:TPU:63, one launch (start us, length us, event | category | flops | bytes accessed | tf_op | source)
XLA Modules:
  0.0 81.0 jit_solution(7379606361308435332)
XLA Ops:
  0.0 79.6 %shard_map.73 = bf16[128,128]{1,0:T(8,128)(2,1)} custom-call(bf16[16,8,32,128]{3,2,1,0:T(8,128)(2,1)} %bitcast.13, bf16[8,2048]{1,0:T(8,128)(2,1)} %bitcast.15, bf16[16,128]{1,0:T(8,128)(2,1)} %bitcast.16, bf16[8,2048]{1,0:T(8,128)(2,1)} %refs_3_.1, s32[1,128]{1,0:T(1,128)} %bitcast.17, s32[8]{0:T(128)} %refs_5_.1, s32[8]{0:T(128)} %refs_6_.1), custom_call_target="tpu_custom_call" | custom-call | tf_op jit(solution)/shard_map/pallas_call | solution.py:423
  79.6 1.4 %copy.10 = bf16[1,8,2048]{2,1,0:T(8,128)(2,1)} copy(bf16[1,8,2048]{2,1,0:T(8,128)(2,1)} %bitcast.14) | data formatting | bytes 65536
